TPU v7x, 512 devices: a whole 4x8x8 slice. The times are simulated.
512 devices in a mesh: dp: 32 (over x_lo, y, core), bfly: 16 (over z, x_hi).
Axes of the slice: x: 4 (x_hi: 2, x_lo: 2; x = x_hi * 2 + x_lo), y: 8, z: 8, core: 2. Of those that a mesh axis runs over, the one named last changes fastest.
Arguments:
- tokens: bfloat16 [8192, 16384], P('dp', 'bfly'), may hold values from -6 to 6
- weight_a: bfloat16 [2, 64, 256, 256], P(None, 'bfly'), may hold values from -0.25 to 0.25
- weight_b: bfloat16 [2, 64, 256, 256], P(None, 'bfly'), may hold values from -0.25 to 0.25
- upstream: bfloat16 [8192, 16384], P('dp', 'bfly'), may hold values from -6 to 6
Outputs:
- output: bfloat16 [8192, 16384], P('dp', 'bfly')
- grad_input: bfloat16 [8192, 16384], P('dp', 'bfly')
- grad_weight_a: float32 [256, 2, 64, 256], P('dp', None, 'bfly')
- grad_weight_b: float32 [256, 2, 64, 256], P('dp', None, 'bfly')
All inputs are finite; a program needn't handle non-finite values.
Results may differ from a plain program's by a relative error of at most 0.005.
Values may be sent and summed in bfloat16 or wider, within the bound.
A program may use at most 64 MiB of HBM per device.

v0:
```python
import jax
import jax.numpy as jnp
from jax import lax
from jax.sharding import PartitionSpec as P


def from_partner(value, axis, apart):
    mask = 2**apart
    pairs = [(source, source ^ mask) for source in range(lax.axis_size(axis))]
    return lax.ppermute(value, axis, pairs)


def activate(values):
    return jax.nn.gelu(values, approximate=False)


def forward_mix(own, other, weights):
    return jnp.einsum(
        "tir,irc->tic", own, weights[0], preferred_element_type=jnp.float32
    ) + jnp.einsum("tir,irc->tic", other, weights[1], preferred_element_type=jnp.float32)


def transpose_mix(grads, weights):
    return jnp.einsum("tic,irc->tir", grads, weights, preferred_element_type=jnp.float32)


def shards(tokens, weight_a, weight_b, upstream):
    tok_rows = tokens.shape[0]
    blocks_dev = weight_a.shape[1]
    block_size = weight_a.shape[2]
    top_bit = lax.axis_size("bfly").bit_length() - 2
    inputs = tokens.reshape(tok_rows, blocks_dev, block_size)
    grads_out = upstream.reshape(tok_rows, blocks_dev, block_size)
    partner_in = from_partner(inputs, "bfly", top_bit)
    pre_act = forward_mix(inputs, partner_in, weight_a)
    hidden = activate(pre_act).astype(jnp.bfloat16)
    partner_hidden = from_partner(hidden, "bfly", 0)
    output = (
        forward_mix(hidden, partner_hidden, weight_b).astype(jnp.bfloat16).reshape(tok_rows, -1)
    )
    remote_term = from_partner(transpose_mix(grads_out, weight_b[1]), "bfly", 0)
    grad_hidden = transpose_mix(grads_out, weight_b[0]) + remote_term
    pull = jax.vjp(activate, pre_act)[1]
    grad_pre = pull(grad_hidden)[0].astype(jnp.bfloat16)
    remote_input = from_partner(transpose_mix(grad_pre, weight_a[1]), "bfly", top_bit)
    grad_in = transpose_mix(grad_pre, weight_a[0]) + remote_input
    grad_input = grad_in.astype(jnp.bfloat16).reshape(tok_rows, -1)
    norm_scale = jnp.float32(tok_rows * lax.axis_size("dp")) ** (-0.5)
    own = hidden
    other = partner_hidden
    first = jnp.einsum("tir,tic->ric", own, grads_out, preferred_element_type=jnp.float32)
    second = jnp.einsum("tir,tic->ric", other, grads_out, preferred_element_type=jnp.float32)
    grad_b = lax.psum_scatter(
        jnp.stack([first, second], 1) * norm_scale, "dp", scatter_dimension=0, tiled=True
    )
    own = inputs
    other = partner_in
    first = jnp.einsum("tir,tic->ric", own, grad_pre, preferred_element_type=jnp.float32)
    second = jnp.einsum("tir,tic->ric", other, grad_pre, preferred_element_type=jnp.float32)
    grad_a = lax.psum_scatter(
        jnp.stack([first, second], 1) * norm_scale, "dp", scatter_dimension=0, tiled=True
    )
    return (output, grad_input, grad_a, grad_b)


def solution(mesh):
    in_specs = (
        P("dp", "bfly"),
        P(None, "bfly", None, None),
        P(None, "bfly", None, None),
        P("dp", "bfly"),
    )
    out_specs = (
        P("dp", "bfly"),
        P("dp", "bfly"),
        P("dp", None, "bfly", None),
        P("dp", None, "bfly", None),
    )
    return jax.shard_map(shards, mesh=mesh, in_specs=in_specs, out_specs=out_specs, check_vma=False)
```

profile of v0, /device:TPU:1, one launch (start us, length us, event | category | flops | bytes accessed | tf_op | source)
XLA Modules:
  0.0 319.5 jit_solution(14213181304269367928)
XLA Ops:
  7.2 1.4 copy.59
  8.6 1.0 copy.62
  9.6 11.5 %collective-permute-start = (bf16[256,4,256]{2,0,1:T(8,128)(2,1)}, bf16[256,4,256]{2,0,1:T(8,128)(2,1)S(1)}, u32[]{:S(2)}, u32[]{:S(2)}) collective-permute-start(bf16[256,4,256]{2,0,1:T(8,128)(2,1)} %copy.62), channel_id=1, source_target_pairs={{0,8},{1,9},{2,10},{3,11},{4,12},{5,13},{6,14},{7,15},{8,0},{9,1},... | collective-permute-start | bytes 1572872 | tf_op jit(solution)/shard_map/ppermute | solution.py:10
  21.1 0.3 convolution_bitcast_fusion.6
  21.5 4.6 %collective-permute-start.2 = (f32[256,4,256]{0,2,1:T(8,128)S(1)}, f32[256,4,256]{0,2,1:T(8,128)S(1)}, u32[]{:S(2)}, u32[]{:S(2)}) collective-permute-start(f32[256,4,256]{0,2,1:T(8,128)S(1)} %convolution_bitcast_fusion.6), channel_id=1, source_target_pairs={{0,1},{1,0},{2,3},{3,2},{4,5},{5,4},{6,7},{7,6},{8,9},{9,8},{10,11... | collective-permute-start | bytes 3145736 | tf_op jit(solution)/shard_map/ppermute | solution.py:10
  26.1 0.3 fusion.37
  26.5 5.7 %collective-permute-done = bf16[256,4,256]{2,0,1:T(8,128)(2,1)S(1)} collective-permute-done((bf16[256,4,256]{2,0,1:T(8,128)(2,1)}, bf16[256,4,256]{2,0,1:T(8,128)(2,1)S(1)}, u32[]{:S(2)}, u32[]{:S(2)}) %collective-permute-start) | collective-permute-done | bytes 524320 | tf_op jit(solution)/shard_map/ppermute | solution.py:10
  32.1 3.4 %fusion.6 = (bf16[256,4,256]{0,2,1:T(8,128)(2,1)}, f32[256,4,256]{0,2,1:T(8,128)S(1)}, f32[4,256,256]{2,1,0:T(8,128)S(1)}) fusion(f32[4,256,256]{2,1,0:T(8,128)S(1)} %fusion.37, bf16[256,4,256]{2,0,1:T(8,128)(2,1)S(1)} %collective-permute-done, bf16[2,4,256,256]{3,2,1,0:T(8,128)(2,1)S(1)} %copy-done.4), kind=kOutput, calls=%fused_computation.25 | convolution fusion | flops 151519232 | bytes 4718592 | tf_op jit(solution)/shard_map/tir,irc->tic/dot_general | solution.py:20
  35.5 5.6 %collective-permute-start.1 = (bf16[256,4,256]{0,2,1:T(8,128)(2,1)}, bf16[256,4,256]{0,2,1:T(8,128)(2,1)}, u32[]{:S(2)}, u32[]{:S(2)}) collective-permute-start(bf16[256,4,256]{0,2,1:T(8,128)(2,1)} %get-tuple-element.18), channel_id=1, source_target_pairs={{0,1},{1,0},{2,3},{3,2},{4,5},{5,4},{6,7},{7,6},{8,9},{9,8},{10,11... | collective-permute-start | bytes 1572872 | tf_op jit(solution)/shard_map/ppermute | solution.py:10
  41.1 2.4 convolution_bitcast_fusion.3
  43.4 5.1 %collective-permute-done.2 = f32[256,4,256]{0,2,1:T(8,128)S(1)} collective-permute-done((f32[256,4,256]{0,2,1:T(8,128)S(1)}, f32[256,4,256]{0,2,1:T(8,128)S(1)}, u32[]{:S(2)}, u32[]{:S(2)}) %collective-permute-start.2) | collective-permute-done | bytes 1048608 | tf_op jit(solution)/shard_map/ppermute | solution.py:10
  48.6 0.7 fusion.12
  49.2 0.3 convolution_bitcast_fusion.5
  49.6 0.3 convolution_bitcast_fusion.4
  49.9 0.2 maximum_multiply_fusion
  50.1 2.0 copy.77
  52.1 7.8 %collective-permute-done.1 = bf16[256,4,256]{0,2,1:T(8,128)(2,1)} collective-permute-done((bf16[256,4,256]{0,2,1:T(8,128)(2,1)}, bf16[256,4,256]{0,2,1:T(8,128)(2,1)}, u32[]{:S(2)}, u32[]{:S(2)}) %collective-permute-start.1) | collective-permute-done | bytes 524320 | tf_op jit(solution)/shard_map/ppermute | solution.py:10
  59.9 1.4 convolution_bitcast_fusion.2
  61.3 0.2 maximum_multiply_fusion.1
  61.5 2.0 copy.82
  63.5 1.2 copy-done.5
  64.7 1.4 convolution_bitcast_fusion
  66.1 1.9 collective-permute-start.3
  68.0 1.3 dynamic-slice
  70.0 1.4 fusion.32
  71.4 1.4 fusion.2
  72.8 1.0 copy.83
  73.8 21.4 %collective-permute-done.3 = f32[256,4,256]{0,2,1:T(8,128)} collective-permute-done((f32[256,4,256]{0,2,1:T(8,128)}, f32[256,4,256]{0,2,1:T(8,128)}, u32[]{:S(2)}, u32[]{:S(2)}) %collective-permute-start.3) | collective-permute-done | bytes 1048608 | tf_op jit(solution)/shard_map/ppermute | solution.py:10
  95.1 1.5 fusion.3
  96.7 1.0 copy.84
  97.7 213.4 %all-reduce.5.cloned.1.call-done = (f32[256,2,4,256]{3,2,1,0:T(4,128)}, f32[256,2,4,256]{3,2,1,0:T(4,128)}) async-done(((f32[256,2,4,256]{3,2,1,0:T(4,128)}, f32[256,2,4,256]{3,2,1,0:T(4,128)}), (f32[256,2,4,256]{3,2,1,0:T(4,128)}, f32[256,2,4,256]{3,2,1,0:T(4,128)})) %all-reduce.5.cloned.1.call-update) | async-done | bytes 4194320
  311.1 1.5 constant_dynamic-slice_fusion
  (13 shorter events, 0.1 us)
Async XLA Ops:
  7.2 13.9 %copy-start.2 = (bf16[2,4,256,256]{3,2,1,0:T(8,128)(2,1)S(1)}, bf16[2,4,256,256]{3,2,1,0:T(8,128)(2,1)}, u32[]{:S(2)}) copy-start(bf16[2,4,256,256]{3,2,1,0:T(8,128)(2,1)} %param.6) | copy-start | bytes 3145732
  7.2 13.9 %copy-start = (bf16[256,1024]{1,0:T(8,128)(2,1)S(1)}, bf16[256,1024]{1,0:T(8,128)(2,1)}, u32[]{:S(2)}) copy-start(bf16[256,1024]{1,0:T(8,128)(2,1)} %param.7) | copy-start | bytes 1572868
  7.2 18.9 %copy-start.4 = (bf16[2,4,256,256]{3,2,1,0:T(8,128)(2,1)S(1)}, bf16[2,4,256,256]{3,2,1,0:T(8,128)(2,1)}, u32[]{:S(2)}) copy-start(bf16[2,4,256,256]{3,2,1,0:T(8,128)(2,1)} %param.5) | copy-start | bytes 3145732
  7.2 303.9 %all-reduce.5.cloned.1.call-start = ((), (), s32[]{:S(2)}) async-start(), calls=%async_computation | async-start | bytes 8388608
  9.6 22.5 %collective-permute-start = (bf16[256,4,256]{2,0,1:T(8,128)(2,1)}, bf16[256,4,256]{2,0,1:T(8,128)(2,1)S(1)}, u32[]{:S(2)}, u32[]{:S(2)}) collective-permute-start(bf16[256,4,256]{2,0,1:T(8,128)(2,1)} %copy.62), channel_id=1, source_target_pairs={{0,8},{1,9},{2,10},{3,11},{4,12},{5,13},{6,14},{7,15},{8,0},{9,1},... | collective-permute-start | bytes 1572872 | tf_op jit(solution)/shard_map/ppermute | solution.py:10
  21.5 27.1 %collective-permute-start.2 = (f32[256,4,256]{0,2,1:T(8,128)S(1)}, f32[256,4,256]{0,2,1:T(8,128)S(1)}, u32[]{:S(2)}, u32[]{:S(2)}) collective-permute-start(f32[256,4,256]{0,2,1:T(8,128)S(1)} %convolution_bitcast_fusion.6), channel_id=1, source_target_pairs={{0,1},{1,0},{2,3},{3,2},{4,5},{5,4},{6,7},{7,6},{8,9},{9,8},{10,11... | collective-permute-start | bytes 3145736 | tf_op jit(solution)/shard_map/ppermute | solution.py:10
  35.5 24.4 %collective-permute-start.1 = (bf16[256,4,256]{0,2,1:T(8,128)(2,1)}, bf16[256,4,256]{0,2,1:T(8,128)(2,1)}, u32[]{:S(2)}, u32[]{:S(2)}) collective-permute-start(bf16[256,4,256]{0,2,1:T(8,128)(2,1)} %get-tuple-element.18), channel_id=1, source_target_pairs={{0,1},{1,0},{2,3},{3,2},{4,5},{5,4},{6,7},{7,6},{8,9},{9,8},{10,11... | collective-permute-start | bytes 1572872 | tf_op jit(solution)/shard_map/ppermute | solution.py:10
  52.1 9.2 %copy-start.1 = (f32[256,1,4,256]{0,3,2,1:T(8,128)S(1)}, f32[256,1,4,256]{0,3,2,1:T(8,128)}, u32[]{:S(2)}) copy-start(f32[256,1,4,256]{0,3,2,1:T(8,128)} %convolution_bitcast_fusion.3) | copy-start | bytes 3145732
  63.5 1.2 copy-start.5
  64.7 5.2 %copy-start.3 = (bf16[2,4,256,256]{3,2,1,0:T(8,128)(2,1)S(1)}, bf16[2,4,256,256]{3,2,1,0:T(8,128)(2,1)}, u32[]{:S(2)}) copy-start(bf16[2,4,256,256]{3,2,1,0:T(8,128)(2,1)} %param.6) | copy-start | bytes 3145732
  66.1 29.0 %collective-permute-start.3 = (f32[256,4,256]{0,2,1:T(8,128)}, f32[256,4,256]{0,2,1:T(8,128)}, u32[]{:S(2)}, u32[]{:S(2)}) collective-permute-start(f32[256,4,256]{0,2,1:T(8,128)} %convolution_bitcast_fusion), channel_id=1, source_target_pairs={{0,8},{1,9},{2,10},{3,11},{4,12},{5,13},{6,14},{7,15},{8,0},{9,1},... | collective-permute-start | bytes 3145736 | tf_op jit(solution)/shard_map/ppermute | solution.py:10
Sparse Core Ops, SparseCore 0:
  63.7 247.4 all-reduce.4
where the time goes:
time: 320 us; the launch traced here: 319 us
  waiting for transfers between devices  253 us (79%)
  starting transfers between devices  23.6 us (7%)
  between operations  14.9 us (5%)
  matrix products  14.8 us (5%)
  local copies, waits for them, and re-layouts  12.4 us (4%)
    unnamed x2, waiting for transfers between devices  213 us
    ppermute x4, waiting for transfers between devices, from_partner(): return lax.ppermute(value, axis, pairs)  40 us
    ppermute x4, starting transfers between devices, from_partner(): return lax.ppermute(value, axis, pairs)  23.6 us
    unnamed x17, local copies, waits for them, and re-layouts  7.42 us
  transfers between devices with their start and end apart: 5, of which 5 were waited for; matrix products, arithmetic and copies ran while one was open for 6% of the time, Pallas kernels for 0%

commit v1 on v0

v1 whole, which is shorter than its diff:
```python
import functools

import jax
import jax.numpy as jnp
from jax import lax
from jax.experimental import pallas as pl
from jax.experimental.pallas import tpu as pltpu
from jax.sharding import PartitionSpec as P

MESH = pl.DeviceIdType.MESH
NY = 8
NZ = 8
F32 = jnp.float32
BF16 = jnp.bfloat16
ROWS = 32


def dot_nn(a, b):
    return lax.dot_general(a, b, (((1,), (0,)), ((), ())), preferred_element_type=F32)


def dot_nt(a, b):
    return lax.dot_general(a, b, (((1,), (1,)), ((), ())), preferred_element_type=F32)


def dot_tn(a, b):
    return lax.dot_general(a, b, (((0,), (0,)), ((), ())), preferred_element_type=F32)


def main_kernel(
    scale,
    x_hbm,
    g_hbm,
    wa_hbm,
    wb_hbm,
    out_hbm,
    gi_hbm,
    ga_hbm,
    gb_hbm,
    xv,
    gv,
    wav,
    wbv,
    xp,
    ps,
    pr,
    hv,
    hp,
    cs,
    cr,
    uf,
    dhf,
    du,
    own,
    loc,
    sib,
    ysend,
    yrecv,
    tsum,
    trecv,
    outv,
    giv,
    gav,
    gbv,
    load_sem,
    store_sem,
    x_ss,
    x_rs,
    p_ss,
    p_rs,
    h_ss,
    h_rs,
    c_ss,
    c_rs,
    m_ss,
    m_rs,
    y_ss,
    y_rs,
    t_ss,
    t_rs,
):
    n_blk, size = xv.shape[0], xv.shape[1]
    dp, bfly = lax.axis_index("dp"), lax.axis_index("bfly")
    core, y, xl = dp % 2, (dp // 2) % NY, dp // (2 * NY)
    z, xh = bfly // 2, bfly % 2
    z_dev = (dp, ((z + NZ // 2) % NZ) * 2 + xh)
    xh_dev = (dp, z * 2 + (1 - xh))
    core_dev = (dp + 1 - 2 * core, bfly)
    xl_dev = (((1 - xl) * NY + y) * 2 + core, bfly)

    def y_dev(to):
        return ((xl * NY + to) * 2 + core, bfly)

    def remote(src, dst, ss, rs, dev):
        return pltpu.make_async_remote_copy(
            src_ref=src, dst_ref=dst, send_sem=ss, recv_sem=rs, device_id=dev, device_id_type=MESH
        )

    def cols(k):
        return pl.ds(k * size, size)

    load_g = [pltpu.make_async_copy(g_hbm.at[:, cols(k)], gv.at[k], load_sem.at[k]) for k in range(n_blk)]
    load_x = [
        pltpu.make_async_copy(x_hbm.at[:, cols(k)], xv.at[k], load_sem.at[n_blk + k]) for k in range(n_blk)
    ]
    load_wb = [pltpu.make_async_copy(wb_hbm.at[s], wbv.at[s], load_sem.at[2 * n_blk + s]) for s in range(2)]
    load_wa = [pltpu.make_async_copy(wa_hbm.at[s], wav.at[s], load_sem.at[2 * n_blk + 2 + s]) for s in range(2)]
    load_wb[1].start()
    for c in load_g:
        c.start()
    for c in load_x:
        c.start()
    load_wa[0].start()
    load_wb[0].start()
    load_wa[1].start()

    barrier = pltpu.get_barrier_semaphore()
    for dev in [z_dev, xh_dev, core_dev, xl_dev] + [y_dev((y + j) % NY) for j in range(1, NY)]:
        pl.semaphore_signal(barrier, inc=1, device_id=dev, device_id_type=MESH)

    load_wb[1].wait()
    for k in range(n_blk):
        load_g[k].wait()
        ps[k] = dot_nt(gv[k], wbv[1, k]).astype(BF16)

    pl.semaphore_wait(barrier, 3 + NY)

    send_x = [remote(x_hbm.at[:, cols(k)], xp.at[k], x_ss.at[k], x_rs.at[k], z_dev) for k in range(n_blk)]
    send_p = [remote(ps.at[k], pr.at[k], p_ss.at[k], p_rs.at[k], xh_dev) for k in range(n_blk)]
    for c in send_x:
        c.start()
    for c in send_p:
        c.start()
    send_h = [remote(hv.at[k], hp.at[k], h_ss.at[k], h_rs.at[k], xh_dev) for k in range(n_blk)]
    send_c = [remote(cs.at[k], cr.at[k], c_ss.at[k], c_rs.at[k], z_dev) for k in range(n_blk)]
    send_m = [
        [
            remote(
                loc.at[k, pl.ds(2 * h, 2), :, :, 1 - core],
                sib.at[k, pl.ds(2 * h, 2)],
                m_ss.at[k, h],
                m_rs.at[k, h],
                core_dev,
            )
            for h in range(2)
        ]
        for k in range(n_blk)
    ]
    send_y = [
        [
            remote(
                ysend.at[k, (y + j) % NY],
                yrecv.at[k, j - 1],
                y_ss.at[k, j - 1],
                y_rs.at[k, j - 1],
                y_dev((y + j) % NY),
            )
            for j in range(1, NY)
        ]
        for k in range(n_blk)
    ]
    send_t = [remote(tsum.at[k, 1 - xl], trecv.at[k], t_ss.at[k], t_rs.at[k], xl_dev) for k in range(n_blk)]
    store_out = [
        pltpu.make_async_copy(outv.at[k], out_hbm.at[:, cols(k)], store_sem.at[k]) for k in range(n_blk)
    ]
    store_gi = [
        pltpu.make_async_copy(giv.at[k], gi_hbm.at[:, cols(k)], store_sem.at[n_blk + k]) for k in range(n_blk)
    ]
    store_ga = pltpu.make_async_copy(gav, ga_hbm, store_sem.at[2 * n_blk])
    store_gb = pltpu.make_async_copy(gbv, gb_hbm, store_sem.at[2 * n_blk + 1])

    def keep(k, m, value):
        loc[k, m] = value.reshape(loc.shape[2:])

    def first_factor(k):
        load_x[k].wait()
        if k == 0:
            load_wa[0].wait()
            load_wa[1].wait()
            load_wb[0].wait()
        dhf[...] = dot_nt(gv[k], wbv[0, k])
        uf[...] = dot_nn(xv[k], wav[0, k])
        send_x[k].wait_recv()
        uf[...] += dot_nn(xp[k], wav[1, k])
        send_p[k].wait_recv()

        def rows(i, _):
            at = pl.ds(pl.multiple_of(i * ROWS, ROWS), ROWS)
            u = uf[at, :]
            dh = dhf[at, :] + pr[k, at, :].astype(F32)
            phi = 0.5 + 0.5 * lax.erf(u * F32(0.5**0.5))
            dens = jnp.exp(u * u * F32(-0.5)) * F32(0.3989422804014327)
            hv[k, at, :] = (u * phi).astype(BF16)
            du[k, at, :] = (dh * (phi + u * dens)).astype(BF16)
            return 0

        lax.fori_loop(0, size // ROWS, rows, 0)
        send_h[k].start()
        cs[k] = dot_nt(du[k], wav[1, k]).astype(BF16)
        send_c[k].start()
        keep(k, 0, dot_tn(xv[k], du[k]))
        keep(k, 1, dot_tn(xp[k], du[k]))
        send_m[k][0].start()
        own[k] = dot_nt(du[k], wav[0, k])

    def second_factor(k):
        keep(k, 2, dot_tn(hv[k], gv[k]))
        mine = dot_nn(hv[k], wbv[0, k])
        send_h[k].wait_recv()
        keep(k, 3, dot_tn(hp[k], gv[k]))
        send_m[k][1].start()
        outv[k] = (mine + dot_nn(hp[k], wbv[1, k])).astype(BF16)
        store_out[k].start()

    def to_owners(k):
        for h in range(2):
            send_m[k][h].wait_recv()
        for m in range(4):
            both = [loc[k, m, s, :, core] + sib[k, m, s] for s in range(2)]
            ysend[k, :, m] = jnp.concatenate(both, axis=1).astype(BF16)
        for j in (4, 3, 5, 2, 6, 1, 7):
            send_y[k][j - 1].start()

    def sum_y(k):
        for j in range(1, NY):
            send_y[k][j - 1].wait_recv()
        for m in range(4):
            mine = [loc[k, m, s, y, core] + sib[k, m, s, y] for s in range(2)]
            total = jnp.concatenate(mine, axis=0)
            for j in range(NY - 1):
                total = total + yrecv[k, j, m].astype(F32)
            tsum[k, 0, m] = total[:8]
            tsum[k, 1, m] = total[8:]
        send_t[k].start()

    def finish_weights(k):
        send_t[k].wait_recv()
        for m in range(4):
            value = (tsum[k, xl, m] + trecv[k, m]) * scale
            into = gav if m < 2 else gbv
            for r in range(8):
                into[r, m % 2, pl.ds(k, 1), :] = value[r : r + 1, :]

    def finish_input(k):
        send_c[k].wait_recv()
        giv[k] = (own[k] + cr[k].astype(F32)).astype(BF16)
        store_gi[k].start()

    first_factor(0)
    first_factor(1)
    second_factor(0)
    first_factor(2)
    second_factor(1)
    to_owners(0)
    first_factor(3)
    second_factor(2)
    to_owners(1)
    sum_y(0)
    second_factor(3)
    to_owners(2)
    sum_y(1)
    finish_weights(0)
    to_owners(3)
    sum_y(2)
    finish_weights(1)
    finish_input(0)
    sum_y(3)
    finish_weights(2)
    finish_input(1)
    finish_weights(3)
    store_ga.start()
    store_gb.start()
    finish_input(2)
    for k in range(n_blk):
        for c in [send_x[k], send_p[k], send_h[k], *send_m[k], *send_y[k], send_t[k]]:
            c.wait_send()
        store_out[k].wait()
    store_ga.wait()
    store_gb.wait()
    finish_input(3)
    for k in range(n_blk):
        send_c[k].wait_send()
        store_gi[k].wait()


def copy_kernel(*refs):
    n = len(refs) // 2
    sems = refs[-1]
    copies = [pltpu.make_async_copy(refs[i], refs[n + i], sems.at[i]) for i in range(n)]
    for c in copies:
        c.start()
    for c in copies:
        c.wait()


def shards(n_dp, tokens, weight_a, weight_b, upstream):
    rows, width = tokens.shape
    n_blk, size = weight_a.shape[1], weight_a.shape[2]
    own_rows = size // n_dp
    scale = float((rows * n_dp) ** -0.5)
    results = (
        jax.ShapeDtypeStruct((rows, width), BF16),
        jax.ShapeDtypeStruct((rows, width), BF16),
        jax.ShapeDtypeStruct((own_rows, 2, n_blk, size), F32),
        jax.ShapeDtypeStruct((own_rows, 2, n_blk, size), F32),
    )
    anywhere = pl.BlockSpec(memory_space=pl.ANY)
    act = pltpu.VMEM((n_blk, rows, size), BF16)
    weights = pltpu.VMEM((2, n_blk, size, size), BF16)
    dma = pltpu.SemaphoreType.DMA
    made = pl.pallas_call(
        functools.partial(main_kernel, scale),
        out_shape=results,
        in_specs=[anywhere] * 4,
        out_specs=[anywhere] * 4,
        scratch_shapes=[
            act,
            act,
            weights,
            weights,
            act,
            act,
            act,
            act,
            act,
            act,
            act,
            pltpu.VMEM((rows, size), F32),
            pltpu.VMEM((rows, size), F32),
            act,
            pltpu.VMEM((n_blk, rows, size), F32),
            pltpu.VMEM((n_blk, 4, 2, NY, 2, own_rows, size), F32),
            pltpu.VMEM((n_blk, 4, 2, NY, own_rows, size), F32),
            pltpu.VMEM((n_blk, NY, 4, 2 * own_rows, size), BF16),
            pltpu.VMEM((n_blk, NY - 1, 4, 2 * own_rows, size), BF16),
            pltpu.VMEM((n_blk, 2, 4, own_rows, size), F32),
            pltpu.VMEM((n_blk, 4, own_rows, size), F32),
            act,
            act,
            pltpu.VMEM((own_rows, 2, n_blk, size), F32),
            pltpu.VMEM((own_rows, 2, n_blk, size), F32),
            dma((2 * n_blk + 4,)),
            dma((2 * n_blk + 2,)),
            dma((n_blk,)),
            dma((n_blk,)),
            dma((n_blk,)),
            dma((n_blk,)),
            dma((n_blk,)),
            dma((n_blk,)),
            dma((n_blk,)),
            dma((n_blk,)),
            dma((n_blk, 2)),
            dma((n_blk, 2)),
            dma((n_blk, NY - 1)),
            dma((n_blk, NY - 1)),
            dma((n_blk,)),
            dma((n_blk,)),
        ],
        compiler_params=pltpu.CompilerParams(
            collective_id=0, has_side_effects=True, vmem_limit_bytes=48 << 20
        ),
    )(tokens, upstream, weight_a, weight_b)
    return pl.pallas_call(
        copy_kernel,
        out_shape=results,
        in_specs=[anywhere] * 4,
        out_specs=[anywhere] * 4,
        scratch_shapes=[dma((4,))],
    )(*made)


def solution(mesh):
    in_specs = (
        P("dp", "bfly"),
        P(None, "bfly", None, None),
        P(None, "bfly", None, None),
        P("dp", "bfly"),
    )
    out_specs = (
        P("dp", "bfly"),
        P("dp", "bfly"),
        P("dp", None, "bfly", None),
        P("dp", None, "bfly", None),
    )
    return jax.shard_map(
        functools.partial(shards, mesh.shape["dp"]),
        mesh=mesh,
        in_specs=in_specs,
        out_specs=out_specs,
        check_vma=False,
    )
```

time: 320 us -> 123 us (0.38)
  the two profiles are of different devices: /device:TPU:1 before, /device:TPU:128 now
where the time goes in v1:
time: 123 us
  Pallas kernels  115 us (93%)
  local copies, waits for them, and re-layouts  7.37 us (6%)
    pallas_call x1, Pallas kernels, shards(): pl.pallas_call(functools.partial(main_kernel, scale), out_shape=results,...  77.8 us
    pallas_call x1, Pallas kernels, shards(): pl.pallas_call(copy_kernel, out_shape=results, in_specs=[anywhere] * 4, o...  36.9 us
    unnamed x16, local copies, waits for them, and re-layouts  7.37 us

profile of v1, /device:TPU:128, one launch (start us, length us, event | category | flops | bytes accessed | tf_op | source)
XLA Modules:
  0.0 122.7 jit_solution(2066244961500973909)
XLA Ops:
  0.6 0.0 copy-start
  0.6 1.2 copy-done
  1.9 0.0 copy-start.1
  1.9 1.2 copy-done.1
  3.1 0.0 copy-start.4
  3.1 1.0 copy-done.4
  4.1 0.0 copy-start.5
  4.1 1.0 copy-done.5
  5.2 77.8 %shard_map.75 = (bf16[256,1024]{1,0:T(8,128)(2,1)S(1)}, bf16[256,1024]{1,0:T(8,128)(2,1)S(1)}, f32[8,2,4,256]{3,2,1,0:T(4,128)S(1)}, f32[8,2,4,256]{3,2,1,0:T(4,128)S(1)}) custom-call(bf16[256,1024]{1,0:T(8,128)(2,1)S(1)} %copy-done.4, bf16[256,1024]{1,0:T(8,128)(2,1)S(1)} %copy-done.5, bf16[2,4,256,256]{3,2,1,0:T(8,128)(2,1)S(1)} %copy-done, ...), custom_call_target="tpu_custom_call" | custom-call | tf_op jit(solution)/shard_map/pallas_call | solution.py:311
  83.0 0.0 copy-start.2
  83.0 0.8 copy-done.2
  83.8 0.0 copy-start.3
  83.8 0.8 copy-done.3
  84.6 0.0 copy-start.6
  84.6 0.6 copy-done.6
  85.2 0.0 copy-start.7
  85.2 0.6 copy-done.7
  85.8 36.9 %shard_map.76 = (bf16[256,1024]{1,0:T(8,128)(2,1)}, bf16[256,1024]{1,0:T(8,128)(2,1)}, f32[8,2,4,256]{3,2,1,0:T(4,128)}, f32[8,2,4,256]{3,2,1,0:T(4,128)}) custom-call(bf16[256,1024]{1,0:T(8,128)(2,1)} %copy-done.2, bf16[256,1024]{1,0:T(8,128)(2,1)} %copy-done.3, f32[8,2,4,256]{3,2,1,0:T(4,128)} %copy-done.6, f32[8,2,4,256]{3,2,1,0:T(4,128)} %copy-done.7), custom_call_target="tpu_custom_call" | custom-call | tf_op jit(solution)/shard_map/pallas_call | solution.py:363
Async XLA Ops:
  0.6 1.2 copy-start
  1.9 1.2 copy-start.1
  3.1 1.0 copy-start.4
  4.1 1.0 copy-start.5
  83.0 0.8 copy-start.2
  83.8 0.8 copy-start.3
  84.6 0.6 copy-start.6
  85.2 0.6 copy-start.7

commit v2 on v1

--- a/solution.py
+++ b/solution.py
@@ -12,6 +12,7 @@
 NZ = 8
 F32 = jnp.float32
 BF16 = jnp.bfloat16
+SIGNAL_AT = 2
 ROWS = 32
 
 
@@ -78,6 +79,7 @@
     y_rs,
     t_ss,
     t_rs,
+    phase,
 ):
     n_blk, size = xv.shape[0], xv.shape[1]
     dp, bfly = lax.axis_index("dp"), lax.axis_index("bfly")
@@ -88,6 +90,8 @@
     core_dev = (dp + 1 - 2 * core, bfly)
     xl_dev = (((1 - xl) * NY + y) * 2 + core, bfly)
 
+    ring = [(dp, ((z + j) % NZ) * 2 + xh) for j in range(1, NZ)]
+
     def y_dev(to):
         return ((xl * NY + to) * 2 + core, bfly)
 
@@ -115,7 +119,7 @@
     load_wa[1].start()
 
     barrier = pltpu.get_barrier_semaphore()
-    for dev in [z_dev, xh_dev, core_dev, xl_dev] + [y_dev((y + j) % NY) for j in range(1, NY)]:
+    for dev in [xh_dev, core_dev, xl_dev] + ring + [y_dev((y + j) % NY) for j in range(1, NY)]:
         pl.semaphore_signal(barrier, inc=1, device_id=dev, device_id_type=MESH)
 
     load_wb[1].wait()
@@ -123,7 +127,7 @@
         load_g[k].wait()
         ps[k] = dot_nt(gv[k], wbv[1, k]).astype(BF16)
 
-    pl.semaphore_wait(barrier, 3 + NY)
+    pl.semaphore_wait(barrier, 1 + NY + NZ)
 
     send_x = [remote(x_hbm.at[:, cols(k)], xp.at[k], x_ss.at[k], x_rs.at[k], z_dev) for k in range(n_blk)]
     send_p = [remote(ps.at[k], pr.at[k], p_ss.at[k], p_rs.at[k], xh_dev) for k in range(n_blk)]
@@ -181,6 +185,9 @@
         dhf[...] = dot_nt(gv[k], wbv[0, k])
         uf[...] = dot_nn(xv[k], wav[0, k])
         send_x[k].wait_recv()
+        if k == SIGNAL_AT:
+            for dev in ring:
+                pl.semaphore_signal(phase, inc=1, device_id=dev, device_id_type=MESH)
         uf[...] += dot_nn(xp[k], wav[1, k])
         send_p[k].wait_recv()
 
@@ -197,7 +204,6 @@
         lax.fori_loop(0, size // ROWS, rows, 0)
         send_h[k].start()
         cs[k] = dot_nt(du[k], wav[1, k]).astype(BF16)
-        send_c[k].start()
         keep(k, 0, dot_tn(xv[k], du[k]))
         keep(k, 1, dot_tn(xp[k], du[k]))
         send_m[k][0].start()
@@ -255,6 +261,9 @@
     first_factor(3)
     second_factor(2)
     to_owners(1)
+    pl.semaphore_wait(phase, NZ - 1)
+    for c in send_c:
+        c.start()
     sum_y(0)
     second_factor(3)
     to_owners(2)
@@ -283,16 +292,6 @@
         store_gi[k].wait()
 
 
-def copy_kernel(*refs):
-    n = len(refs) // 2
-    sems = refs[-1]
-    copies = [pltpu.make_async_copy(refs[i], refs[n + i], sems.at[i]) for i in range(n)]
-    for c in copies:
-        c.start()
-    for c in copies:
-        c.wait()
-
-
 def shards(n_dp, tokens, weight_a, weight_b, upstream):
     rows, width = tokens.shape
     n_blk, size = weight_a.shape[1], weight_a.shape[2]
@@ -355,18 +354,24 @@
             dma((n_blk, NY - 1)),
             dma((n_blk,)),
             dma((n_blk,)),
+            pltpu.SemaphoreType.REGULAR,
         ],
         compiler_params=pltpu.CompilerParams(
-            collective_id=0, has_side_effects=True, vmem_limit_bytes=48 << 20
+            collective_id=0, has_side_effects=True, vmem_limit_bytes=60 << 20
         ),
     )(tokens, upstream, weight_a, weight_b)
+    vm = pl.BlockSpec(memory_space=pltpu.VMEM)
     return pl.pallas_call(
         copy_kernel,
         out_shape=results,
-        in_specs=[anywhere] * 4,
-        out_specs=[anywhere] * 4,
-        scratch_shapes=[dma((4,))],
+        in_specs=[vm] * 4,
+        out_specs=[vm] * 4,
     )(*made)
+
+
+def copy_kernel(*refs):
+    for i in range(4):
+        refs[4 + i][...] = refs[i][...]
 
 
 def solution(mesh):

time: 123 us -> 70.5 us (0.57)
  Pallas kernels: 115 us -> 69.8 us
  local copies, waits for them, and re-layouts: 7.37 us -> 0 us
    pallas_call x1, Pallas kernels: 36.9 us -> 2.24 us  [shards(): pl.pallas_call(copy_kernel, out_shape=results, in_specs=[vm] * 4, out_spe...]
    pallas_call x1, Pallas kernels: 77.8 us -> 67.5 us  [shards(): pl.pallas_call(functools.partial(main_kernel, scale), out_shape=results,...]
    unnamed x16 -> x0, local copies, waits for them, and re-layouts: 7.37 us -> none
where the time goes in v2:
time: 70.5 us; the launch traced here: 70.4 us
  Pallas kernels  69.8 us (99%)
    pallas_call x1, Pallas kernels, shards(): pl.pallas_call(functools.partial(main_kernel, scale), out_shape=results,...  67.5 us
    pallas_call x1, Pallas kernels, shards(): pl.pallas_call(copy_kernel, out_shape=results, in_specs=[vm] * 4, out_spe...  2.24 us

profile of v2, /device:TPU:128, one launch (start us, length us, event | category | flops | bytes accessed | tf_op | source)
XLA Modules:
  0.0 70.4 jit_solution(10140044211716259427)
XLA Ops:
  0.6 67.5 %shard_map.75 = (bf16[256,1024]{1,0:T(8,128)(2,1)}, bf16[256,1024]{1,0:T(8,128)(2,1)}, f32[8,2,4,256]{3,2,1,0:T(4,128)}, f32[8,2,4,256]{3,2,1,0:T(4,128)}) custom-call(bf16[256,1024]{1,0:T(8,128)(2,1)} %x_hbm.1, bf16[256,1024]{1,0:T(8,128)(2,1)} %g_hbm.1, bf16[2,4,256,256]{3,2,1,0:T(8,128)(2,1)} %wa_hbm.1, bf16[2,4,256,256]{3,2,1,0:T(8,128)(2,1)} %wb_hbm.1), custom_call_target="tpu_custom_call" | custom-call | tf_op jit(solution)/shard_map/pallas_call | solution.py:310
  68.2 2.2 %shard_map.76 = (bf16[256,1024]{1,0:T(8,128)(2,1)}, bf16[256,1024]{1,0:T(8,128)(2,1)}, f32[8,2,4,256]{3,2,1,0:T(4,128)}, f32[8,2,4,256]{3,2,1,0:T(4,128)}) custom-call(bf16[256,1024]{1,0:T(8,128)(2,1)} %get-tuple-element.8.refs_0_, bf16[256,1024]{1,0:T(8,128)(2,1)} %get-tuple-element.9.refs_1_, f32[8,2,4,256]{3,2,1,0:T(4,128)} %get-tuple-element.10.refs_2_, ...), custom_call_target="tpu_custom_call" | custom-call | tf_op jit(solution)/shard_map/pallas_call | solution.py:364

commit v3 on v2

--- a/solution.py
+++ b/solution.py
@@ -38,6 +38,8 @@
     gi_hbm,
     ga_hbm,
     gb_hbm,
+    own_hbm,
+    last_hbm,
     xv,
     gv,
     wav,
@@ -80,6 +82,8 @@
     t_ss,
     t_rs,
     phase,
+    told,
+    go,
 ):
     n_blk, size = xv.shape[0], xv.shape[1]
     dp, bfly = lax.axis_index("dp"), lax.axis_index("bfly")
@@ -102,6 +106,18 @@
 
     def cols(k):
         return pl.ds(k * size, size)
+
+    half = NZ // 2
+    low = z < half
+    plane = [y_dev((y + j) % NY) for j in range(1, NY)] + [xh_dev, xl_dev, core_dev]
+    known = plane + [(dp, ((z + j) % half) * 2 + xh) for j in range(1, half)]
+    barrier = pltpu.get_barrier_semaphore()
+    pl.semaphore_signal(barrier, inc=1, device_id=z_dev, device_id_type=MESH)
+
+    @pl.when(low)
+    def _():
+        for dev in known:
+            pl.semaphore_signal(barrier, inc=1, device_id=dev, device_id_type=MESH)
 
     load_g = [pltpu.make_async_copy(g_hbm.at[:, cols(k)], gv.at[k], load_sem.at[k]) for k in range(n_blk)]
     load_x = [
@@ -118,25 +134,37 @@
     load_wb[0].start()
     load_wa[1].start()
 
-    barrier = pltpu.get_barrier_semaphore()
-    for dev in [xh_dev, core_dev, xl_dev] + ring + [y_dev((y + j) % NY) for j in range(1, NY)]:
-        pl.semaphore_signal(barrier, inc=1, device_id=dev, device_id_type=MESH)
+    pl.semaphore_wait(barrier, jnp.where(low, 1 + len(known), 1))
+
+    send_x = [remote(x_hbm.at[:, cols(k)], xp.at[k], x_ss.at[k], x_rs.at[k], z_dev) for k in range(n_blk)]
+    send_p = [remote(ps.at[k], pr.at[k], p_ss.at[k], p_rs.at[k], xh_dev) for k in range(n_blk)]
+    for c in send_x:
+        c.start()
+    @pl.when(low)
+    def _():
+        for dev in known:
+            pl.semaphore_signal(told, inc=1, device_id=dev, device_id_type=MESH)
 
     load_wb[1].wait()
     for k in range(n_blk):
         load_g[k].wait()
         ps[k] = dot_nt(gv[k], wbv[1, k]).astype(BF16)
 
-    pl.semaphore_wait(barrier, 1 + NY + NZ)
-
-    send_x = [remote(x_hbm.at[:, cols(k)], xp.at[k], x_ss.at[k], x_rs.at[k], z_dev) for k in range(n_blk)]
-    send_p = [remote(ps.at[k], pr.at[k], p_ss.at[k], p_rs.at[k], xh_dev) for k in range(n_blk)]
-    for c in send_x:
-        c.start()
+    @pl.when(jnp.logical_not(low))
+    def _():
+        pl.semaphore_wait(go, 1)
+
     for c in send_p:
         c.start()
+
+    @pl.when(low)
+    def _():
+        pl.semaphore_wait(told, len(known))
+        pl.semaphore_signal(go, inc=1, device_id=z_dev, device_id_type=MESH)
+
     send_h = [remote(hv.at[k], hp.at[k], h_ss.at[k], h_rs.at[k], xh_dev) for k in range(n_blk)]
-    send_c = [remote(cs.at[k], cr.at[k], c_ss.at[k], c_rs.at[k], z_dev) for k in range(n_blk)]
+    land_c = [cr.at[k] for k in range(n_blk - 1)] + [last_hbm]
+    send_c = [remote(cs.at[k], land_c[k], c_ss.at[k], c_rs.at[k], z_dev) for k in range(n_blk)]
     send_m = [
         [
             remote(
@@ -168,9 +196,11 @@
         pltpu.make_async_copy(outv.at[k], out_hbm.at[:, cols(k)], store_sem.at[k]) for k in range(n_blk)
     ]
     store_gi = [
-        pltpu.make_async_copy(giv.at[k], gi_hbm.at[:, cols(k)], store_sem.at[n_blk + k]) for k in range(n_blk)
+        pltpu.make_async_copy(giv.at[k], gi_hbm.at[:, cols(k)], store_sem.at[n_blk + k])
+        for k in range(n_blk - 1)
     ]
     store_ga = pltpu.make_async_copy(gav, ga_hbm, store_sem.at[2 * n_blk])
+    store_own = pltpu.make_async_copy(own.at[n_blk - 1], own_hbm, store_sem.at[2 * n_blk - 1])
     store_gb = pltpu.make_async_copy(gbv, gb_hbm, store_sem.at[2 * n_blk + 1])
 
     def keep(k, m, value):
@@ -204,10 +234,14 @@
         lax.fori_loop(0, size // ROWS, rows, 0)
         send_h[k].start()
         cs[k] = dot_nt(du[k], wav[1, k]).astype(BF16)
+        if k == n_blk - 1:
+            send_c[k].start()
         keep(k, 0, dot_tn(xv[k], du[k]))
         keep(k, 1, dot_tn(xp[k], du[k]))
         send_m[k][0].start()
         own[k] = dot_nt(du[k], wav[0, k])
+        if k == n_blk - 1:
+            store_own.start()
 
     def second_factor(k):
         keep(k, 2, dot_tn(hv[k], gv[k]))
@@ -258,12 +292,12 @@
     first_factor(2)
     second_factor(1)
     to_owners(0)
+    pl.semaphore_wait(phase, NZ - 1)
+    for c in send_c[:3]:
+        c.start()
     first_factor(3)
     second_factor(2)
     to_owners(1)
-    pl.semaphore_wait(phase, NZ - 1)
-    for c in send_c:
-        c.start()
     sum_y(0)
     second_factor(3)
     to_owners(2)
@@ -286,10 +320,12 @@
         store_out[k].wait()
     store_ga.wait()
     store_gb.wait()
-    finish_input(3)
-    for k in range(n_blk):
-        send_c[k].wait_send()
-        store_gi[k].wait()
+    for c in store_gi:
+        c.wait()
+    store_own.wait()
+    for c in send_c:
+        c.wait_send()
+    send_c[3].wait_recv()
 
 
 def shards(n_dp, tokens, weight_a, weight_b, upstream):
@@ -309,9 +345,13 @@
     dma = pltpu.SemaphoreType.DMA
     made = pl.pallas_call(
         functools.partial(main_kernel, scale),
-        out_shape=results,
+        out_shape=(
+            *results,
+            jax.ShapeDtypeStruct((rows, size), F32),
+            jax.ShapeDtypeStruct((rows, size), BF16),
+        ),
         in_specs=[anywhere] * 4,
-        out_specs=[anywhere] * 4,
+        out_specs=[anywhere] * 6,
         scratch_shapes=[
             act,
             act,
@@ -354,6 +394,8 @@
             dma((n_blk, NY - 1)),
             dma((n_blk,)),
             dma((n_blk,)),
+            pltpu.SemaphoreType.REGULAR,
+            pltpu.SemaphoreType.REGULAR,
             pltpu.SemaphoreType.REGULAR,
         ],
         compiler_params=pltpu.CompilerParams(
@@ -364,14 +406,18 @@
     return pl.pallas_call(
         copy_kernel,
         out_shape=results,
-        in_specs=[vm] * 4,
+        in_specs=[vm] * 6,
         out_specs=[vm] * 4,
     )(*made)
 
 
-def copy_kernel(*refs):
-    for i in range(4):
-        refs[4 + i][...] = refs[i][...]
+def copy_kernel(out, gi, ga, gb, own, last, out_to, gi_to, ga_to, gb_to):
+    out_to[...] = out[...]
+    ga_to[...] = ga[...]
+    gb_to[...] = gb[...]
+    done = gi.shape[1] - own.shape[1]
+    gi_to[:, :done] = gi[:, :done]
+    gi_to[:, done:] = (own[...] + last[...].astype(F32)).astype(BF16)
 
 
 def solution(mesh):

time: 70.5 us -> 68.4 us (0.970)
  the two profiles are of different devices: /device:TPU:128 before, /device:TPU:2 now
where the time goes in v3:
time: 68.4 us; the launch traced here: 68.3 us
  Pallas kernels  67.7 us (99%)
    pallas_call x1, Pallas kernels, shards(): pl.pallas_call(functools.partial(main_kernel, scale), out_shape=(*results...  65.3 us
    pallas_call x1, Pallas kernels, shards(): pl.pallas_call(copy_kernel, out_shape=results, in_specs=[vm] * 6, out_spe...  2.39 us

profile of v3, /device:TPU:2, one launch (start us, length us, event | category | flops | bytes accessed | tf_op | source)
XLA Modules:
  0.0 68.3 jit_solution(5555566255987652498)
XLA Ops:
  0.6 65.3 %shard_map.75 = (bf16[256,1024]{1,0:T(8,128)(2,1)}, bf16[256,1024]{1,0:T(8,128)(2,1)}, f32[8,2,4,256]{3,2,1,0:T(4,128)}, f32[8,2,4,256]{3,2,1,0:T(4,128)}, f32[256,256]{1,0:T(8,128)}, /*index=5*/bf16[256,256]{1,0:T(8,128)(2,1)}) custom-call(bf16[256,1024]{1,0:T(8,128)(2,1)} %x_hbm.1, bf16[256,1024]{1,0:T(8,128)(2,1)} %g_hbm.1, ...), custom_call_target="tpu_custom_call" | custom-call | tf_op jit(solution)/shard_map/pallas_call | solution.py:346
  65.9 2.4 %shard_map.76 = (bf16[256,1024]{1,0:T(8,128)(2,1)}, bf16[256,1024]{1,0:T(8,128)(2,1)}, f32[8,2,4,256]{3,2,1,0:T(4,128)}, f32[8,2,4,256]{3,2,1,0:T(4,128)}) custom-call(bf16[256,1024]{1,0:T(8,128)(2,1)} %get-tuple-element.10.out, bf16[256,1024]{1,0:T(8,128)(2,1)} %get-tuple-element.11.gi, f32[8,2,4,256]{3,2,1,0:T(4,128)} %get-tuple-element.12.ga, ...), custom_call_target="tpu_custom_call" | custom-call | tf_op jit(solution)/shard_map/pallas_call | solution.py:406

commit v4 on v3

--- a/solution.py
+++ b/solution.py
@@ -12,7 +12,7 @@
 NZ = 8
 F32 = jnp.float32
 BF16 = jnp.bfloat16
-SIGNAL_AT = 2
+SIGNAL_AT = 0
 ROWS = 32
 
 
@@ -59,7 +59,7 @@
     sib,
     ysend,
     yrecv,
-    tsum,
+    tsend,
     trecv,
     outv,
     giv,
@@ -94,7 +94,7 @@
     core_dev = (dp + 1 - 2 * core, bfly)
     xl_dev = (((1 - xl) * NY + y) * 2 + core, bfly)
 
-    ring = [(dp, ((z + j) % NZ) * 2 + xh) for j in range(1, NZ)]
+    ring = [(dp, ((z + j) % NZ) * 2 + xh) for j in (2, NZ - 2)]
 
     def y_dev(to):
         return ((xl * NY + to) * 2 + core, bfly)
@@ -180,18 +180,24 @@
     ]
     send_y = [
         [
-            remote(
-                ysend.at[k, (y + j) % NY],
-                yrecv.at[k, j - 1],
-                y_ss.at[k, j - 1],
-                y_rs.at[k, j - 1],
-                y_dev((y + j) % NY),
-            )
-            for j in range(1, NY)
+            [
+                remote(
+                    ysend.at[k, h, (y + j) % NY],
+                    yrecv.at[k, h, j - 1],
+                    y_ss.at[k, h, j - 1],
+                    y_rs.at[k, h, j - 1],
+                    y_dev((y + j) % NY),
+                )
+                for j in range(1, NY)
+            ]
+            for h in range(2)
         ]
         for k in range(n_blk)
     ]
-    send_t = [remote(tsum.at[k, 1 - xl], trecv.at[k], t_ss.at[k], t_rs.at[k], xl_dev) for k in range(n_blk)]
+    send_t = [
+        [remote(tsend.at[k, h], trecv.at[k, h], t_ss.at[k, h], t_rs.at[k, h], xl_dev) for h in range(2)]
+        for k in range(n_blk)
+    ]
     store_out = [
         pltpu.make_async_copy(outv.at[k], out_hbm.at[:, cols(k)], store_sem.at[k]) for k in range(n_blk)
     ]
@@ -234,7 +240,7 @@
         lax.fori_loop(0, size // ROWS, rows, 0)
         send_h[k].start()
         cs[k] = dot_nt(du[k], wav[1, k]).astype(BF16)
-        if k == n_blk - 1:
+        if k >= 2:
             send_c[k].start()
         keep(k, 0, dot_tn(xv[k], du[k]))
         keep(k, 1, dot_tn(xp[k], du[k]))
@@ -252,34 +258,34 @@
         outv[k] = (mine + dot_nn(hp[k], wbv[1, k])).astype(BF16)
         store_out[k].start()
 
-    def to_owners(k):
-        for h in range(2):
-            send_m[k][h].wait_recv()
-        for m in range(4):
-            both = [loc[k, m, s, :, core] + sib[k, m, s] for s in range(2)]
-            ysend[k, :, m] = jnp.concatenate(both, axis=1).astype(BF16)
+    def merged(k, h, s, at):
+        return jnp.concatenate(
+            [loc[k, m, s, at, core] + sib[k, m, s, at] for m in (2 * h, 2 * h + 1)], axis=-2
+        )
+
+    def to_half(k, h):
+        send_m[k][h].wait_recv()
+        tsend[k, h] = merged(k, h, 1 - xl, slice(None)).astype(BF16)
+        send_t[k][h].start()
+
+    def to_owners(k, h):
+        send_t[k][h].wait_recv()
+        ysend[k, h] = (merged(k, h, xl, slice(None)) + trecv[k, h].astype(F32)).astype(BF16)
         for j in (4, 3, 5, 2, 6, 1, 7):
-            send_y[k][j - 1].start()
-
-    def sum_y(k):
+            send_y[k][h][j - 1].start()
+
+    def finish_weights(k, h):
         for j in range(1, NY):
-            send_y[k][j - 1].wait_recv()
-        for m in range(4):
-            mine = [loc[k, m, s, y, core] + sib[k, m, s, y] for s in range(2)]
-            total = jnp.concatenate(mine, axis=0)
-            for j in range(NY - 1):
-                total = total + yrecv[k, j, m].astype(F32)
-            tsum[k, 0, m] = total[:8]
-            tsum[k, 1, m] = total[8:]
-        send_t[k].start()
-
-    def finish_weights(k):
-        send_t[k].wait_recv()
-        for m in range(4):
-            value = (tsum[k, xl, m] + trecv[k, m]) * scale
-            into = gav if m < 2 else gbv
+            send_y[k][h][j - 1].wait_recv()
+        total = merged(k, h, xl, y) + trecv[k, h, y].astype(F32)
+        for j in range(NY - 1):
+            total = total + yrecv[k, h, j].astype(F32)
+        total = total * scale
+        into = (gav, gbv)[h]
+        for m in range(2):
             for r in range(8):
-                into[r, m % 2, pl.ds(k, 1), :] = value[r : r + 1, :]
+                at = 8 * m + r
+                into[r, m, pl.ds(k, 1), :] = total[at : at + 1, :]
 
     def finish_input(k):
         send_c[k].wait_recv()
@@ -287,35 +293,47 @@
         store_gi[k].start()
 
     first_factor(0)
+    to_half(0, 0)
     first_factor(1)
+    to_half(1, 0)
+    pl.semaphore_wait(phase, len(ring))
+    for c in send_c[:2]:
+        c.start()
+    first_factor(2)
     second_factor(0)
-    first_factor(2)
+    to_half(2, 0)
+    to_owners(0, 0)
+    to_half(0, 1)
     second_factor(1)
-    to_owners(0)
-    pl.semaphore_wait(phase, NZ - 1)
-    for c in send_c[:3]:
-        c.start()
+    to_owners(1, 0)
     first_factor(3)
+    to_half(1, 1)
+    to_owners(0, 1)
+    to_half(3, 0)
     second_factor(2)
-    to_owners(1)
-    sum_y(0)
+    to_owners(2, 0)
+    to_half(2, 1)
+    to_owners(1, 1)
+    finish_weights(0, 0)
     second_factor(3)
-    to_owners(2)
-    sum_y(1)
-    finish_weights(0)
-    to_owners(3)
-    sum_y(2)
-    finish_weights(1)
+    to_owners(3, 0)
+    to_half(3, 1)
+    to_owners(2, 1)
+    finish_weights(1, 0)
+    finish_weights(0, 1)
+    to_owners(3, 1)
+    finish_weights(2, 0)
     finish_input(0)
-    sum_y(3)
-    finish_weights(2)
+    finish_weights(1, 1)
+    finish_weights(3, 0)
     finish_input(1)
-    finish_weights(3)
+    finish_weights(2, 1)
+    finish_input(2)
+    finish_weights(3, 1)
     store_ga.start()
     store_gb.start()
-    finish_input(2)
     for k in range(n_blk):
-        for c in [send_x[k], send_p[k], send_h[k], *send_m[k], *send_y[k], send_t[k]]:
+        for c in [send_x[k], send_p[k], send_h[k], *send_m[k], *send_y[k][0], *send_y[k][1], *send_t[k]]:
             c.wait_send()
         store_out[k].wait()
     store_ga.wait()
@@ -370,10 +388,10 @@
             pltpu.VMEM((n_blk, rows, size), F32),
             pltpu.VMEM((n_blk, 4, 2, NY, 2, own_rows, size), F32),
             pltpu.VMEM((n_blk, 4, 2, NY, own_rows, size), F32),
-            pltpu.VMEM((n_blk, NY, 4, 2 * own_rows, size), BF16),
-            pltpu.VMEM((n_blk, NY - 1, 4, 2 * own_rows, size), BF16),
-            pltpu.VMEM((n_blk, 2, 4, own_rows, size), F32),
-            pltpu.VMEM((n_blk, 4, own_rows, size), F32),
+            pltpu.VMEM((n_blk, 2, NY, 2 * own_rows, size), BF16),
+            pltpu.VMEM((n_blk, 2, NY - 1, 2 * own_rows, size), BF16),
+            pltpu.VMEM((n_blk, 2, NY, 2 * own_rows, size), BF16),
+            pltpu.VMEM((n_blk, 2, NY, 2 * own_rows, size), BF16),
             act,
             act,
             pltpu.VMEM((own_rows, 2, n_blk, size), F32),
@@ -390,10 +408,10 @@
             dma((n_blk,)),
             dma((n_blk, 2)),
             dma((n_blk, 2)),
-            dma((n_blk, NY - 1)),
-            dma((n_blk, NY - 1)),
-            dma((n_blk,)),
-            dma((n_blk,)),
+            dma((n_blk, 2, NY - 1)),
+            dma((n_blk, 2, NY - 1)),
+            dma((n_blk, 2)),
+            dma((n_blk, 2)),
             pltpu.SemaphoreType.REGULAR,
             pltpu.SemaphoreType.REGULAR,
             pltpu.SemaphoreType.REGULAR,

time: 68.4 us -> 63.1 us (0.923)
  the two profiles are of different devices: /device:TPU:2 before, /device:TPU:1 now
where the time goes in v4:
time: 63.1 us; the launch traced here: 62.3 us
  Pallas kernels  61.6 us (98%)
  between operations  0.64 us (1%)
    pallas_call x1, Pallas kernels, shards(): pl.pallas_call(functools.partial(main_kernel, scale), out_shape=(*results...  59.2 us
    pallas_call x1, Pallas kernels, shards(): pl.pallas_call(copy_kernel, out_shape=results, in_specs=[vm] * 6, out_spe...  2.39 us

profile of v4, /device:TPU:1, one launch (start us, length us, event | category | flops | bytes accessed | tf_op | source)
XLA Modules:
  0.0 62.3 jit_solution(16475801762156520781)
XLA Ops:
  0.6 59.2 %shard_map.75 = (bf16[256,1024]{1,0:T(8,128)(2,1)}, bf16[256,1024]{1,0:T(8,128)(2,1)}, f32[8,2,4,256]{3,2,1,0:T(4,128)}, f32[8,2,4,256]{3,2,1,0:T(4,128)}, f32[256,256]{1,0:T(8,128)}, /*index=5*/bf16[256,256]{1,0:T(8,128)(2,1)}) custom-call(bf16[256,1024]{1,0:T(8,128)(2,1)} %x_hbm.1, bf16[256,1024]{1,0:T(8,128)(2,1)} %g_hbm.1, ...), custom_call_target="tpu_custom_call" | custom-call | tf_op jit(solution)/shard_map/pallas_call | solution.py:364
  59.9 2.4 %shard_map.76 = (bf16[256,1024]{1,0:T(8,128)(2,1)}, bf16[256,1024]{1,0:T(8,128)(2,1)}, f32[8,2,4,256]{3,2,1,0:T(4,128)}, f32[8,2,4,256]{3,2,1,0:T(4,128)}) custom-call(bf16[256,1024]{1,0:T(8,128)(2,1)} %get-tuple-element.10.out, bf16[256,1024]{1,0:T(8,128)(2,1)} %get-tuple-element.11.gi, f32[8,2,4,256]{3,2,1,0:T(4,128)} %get-tuple-element.12.ga, ...), custom_call_target="tpu_custom_call" | custom-call | tf_op jit(solution)/shard_map/pallas_call | solution.py:424

commit v5 on v4

--- a/solution.py
+++ b/solution.py
@@ -12,7 +12,6 @@
 NZ = 8
 F32 = jnp.float32
 BF16 = jnp.bfloat16
-SIGNAL_AT = 0
 ROWS = 32
 
 
@@ -34,12 +33,12 @@
     g_hbm,
     wa_hbm,
     wb_hbm,
-    out_hbm,
-    gi_hbm,
-    ga_hbm,
-    gb_hbm,
-    own_hbm,
-    last_hbm,
+    outv,
+    giv,
+    gav,
+    gbv,
+    ownv,
+    last,
     xv,
     gv,
     wav,
@@ -57,16 +56,15 @@
     own,
     loc,
     sib,
+    asend,
+    arecv,
+    asum,
+    frecv,
     ysend,
     yrecv,
     tsend,
     trecv,
-    outv,
-    giv,
-    gav,
-    gbv,
     load_sem,
-    store_sem,
     x_ss,
     x_rs,
     p_ss,
@@ -77,11 +75,14 @@
     c_rs,
     m_ss,
     m_rs,
+    a_ss,
+    a_rs,
+    f_ss,
+    f_rs,
     y_ss,
     y_rs,
     t_ss,
     t_rs,
-    phase,
     told,
     go,
 ):
@@ -94,7 +95,6 @@
     core_dev = (dp + 1 - 2 * core, bfly)
     xl_dev = (((1 - xl) * NY + y) * 2 + core, bfly)
 
-    ring = [(dp, ((z + j) % NZ) * 2 + xh) for j in (2, NZ - 2)]
 
     def y_dev(to):
         return ((xl * NY + to) * 2 + core, bfly)
@@ -163,7 +163,7 @@
         pl.semaphore_signal(go, inc=1, device_id=z_dev, device_id_type=MESH)
 
     send_h = [remote(hv.at[k], hp.at[k], h_ss.at[k], h_rs.at[k], xh_dev) for k in range(n_blk)]
-    land_c = [cr.at[k] for k in range(n_blk - 1)] + [last_hbm]
+    land_c = [cr.at[k] for k in range(n_blk - 1)] + [last]
     send_c = [remote(cs.at[k], land_c[k], c_ss.at[k], c_rs.at[k], z_dev) for k in range(n_blk)]
     send_m = [
         [
@@ -178,36 +178,26 @@
         ]
         for k in range(n_blk)
     ]
-    send_y = [
+    send_a, send_y = (
         [
             [
                 remote(
-                    ysend.at[k, h, (y + j) % NY],
-                    yrecv.at[k, h, j - 1],
-                    y_ss.at[k, h, j - 1],
-                    y_rs.at[k, h, j - 1],
+                    src.at[k, (y + j) % NY],
+                    dst.at[k, j - 1],
+                    ss.at[k, j - 1],
+                    rs.at[k, j - 1],
                     y_dev((y + j) % NY),
                 )
                 for j in range(1, NY)
             ]
-            for h in range(2)
+            for k in range(n_blk)
         ]
-        for k in range(n_blk)
+        for src, dst, ss, rs in ((asend, arecv, a_ss, a_rs), (ysend, yrecv, y_ss, y_rs))
+    )
+    send_t = [remote(tsend.at[k], trecv.at[k], t_ss.at[k], t_rs.at[k], xl_dev) for k in range(n_blk)]
+    send_f = [
+        remote(asum.at[k, 1 - xl], frecv.at[k], f_ss.at[k], f_rs.at[k], xl_dev) for k in range(n_blk)
     ]
-    send_t = [
-        [remote(tsend.at[k, h], trecv.at[k, h], t_ss.at[k, h], t_rs.at[k, h], xl_dev) for h in range(2)]
-        for k in range(n_blk)
-    ]
-    store_out = [
-        pltpu.make_async_copy(outv.at[k], out_hbm.at[:, cols(k)], store_sem.at[k]) for k in range(n_blk)
-    ]
-    store_gi = [
-        pltpu.make_async_copy(giv.at[k], gi_hbm.at[:, cols(k)], store_sem.at[n_blk + k])
-        for k in range(n_blk - 1)
-    ]
-    store_ga = pltpu.make_async_copy(gav, ga_hbm, store_sem.at[2 * n_blk])
-    store_own = pltpu.make_async_copy(own.at[n_blk - 1], own_hbm, store_sem.at[2 * n_blk - 1])
-    store_gb = pltpu.make_async_copy(gbv, gb_hbm, store_sem.at[2 * n_blk + 1])
 
     def keep(k, m, value):
         loc[k, m] = value.reshape(loc.shape[2:])
@@ -221,9 +211,6 @@
         dhf[...] = dot_nt(gv[k], wbv[0, k])
         uf[...] = dot_nn(xv[k], wav[0, k])
         send_x[k].wait_recv()
-        if k == SIGNAL_AT:
-            for dev in ring:
-                pl.semaphore_signal(phase, inc=1, device_id=dev, device_id_type=MESH)
         uf[...] += dot_nn(xp[k], wav[1, k])
         send_p[k].wait_recv()
 
@@ -245,9 +232,10 @@
         keep(k, 0, dot_tn(xv[k], du[k]))
         keep(k, 1, dot_tn(xp[k], du[k]))
         send_m[k][0].start()
-        own[k] = dot_nt(du[k], wav[0, k])
-        if k == n_blk - 1:
-            store_own.start()
+        if k < n_blk - 1:
+            own[k] = dot_nt(du[k], wav[0, k])
+        else:
+            ownv[...] = dot_nt(du[k], wav[0, k])
 
     def second_factor(k):
         keep(k, 2, dot_tn(hv[k], gv[k]))
@@ -255,33 +243,54 @@
         send_h[k].wait_recv()
         keep(k, 3, dot_tn(hp[k], gv[k]))
         send_m[k][1].start()
-        outv[k] = (mine + dot_nn(hp[k], wbv[1, k])).astype(BF16)
-        store_out[k].start()
+        outv[:, cols(k)] = (mine + dot_nn(hp[k], wbv[1, k])).astype(BF16)
 
     def merged(k, h, s, at):
         return jnp.concatenate(
             [loc[k, m, s, at, core] + sib[k, m, s, at] for m in (2 * h, 2 * h + 1)], axis=-2
         )
 
-    def to_half(k, h):
-        send_m[k][h].wait_recv()
-        tsend[k, h] = merged(k, h, 1 - xl, slice(None)).astype(BF16)
-        send_t[k][h].start()
-
-    def to_owners(k, h):
-        send_t[k][h].wait_recv()
-        ysend[k, h] = (merged(k, h, xl, slice(None)) + trecv[k, h].astype(F32)).astype(BF16)
+    def a_to_owners(k):
+        send_m[k][0].wait_recv()
+        halves = [merged(k, 0, s, slice(None)) for s in range(2)]
+        asend[k] = jnp.concatenate(halves, axis=1).astype(BF16)
         for j in (4, 3, 5, 2, 6, 1, 7):
-            send_y[k][h][j - 1].start()
-
-    def finish_weights(k, h):
+            send_a[k][j - 1].start()
+
+    def a_sum(k):
         for j in range(1, NY):
-            send_y[k][h][j - 1].wait_recv()
-        total = merged(k, h, xl, y) + trecv[k, h, y].astype(F32)
+            send_a[k][j - 1].wait_recv()
+        total = jnp.concatenate([merged(k, 0, s, y) for s in range(2)], axis=0)
         for j in range(NY - 1):
-            total = total + yrecv[k, h, j].astype(F32)
+            total = total + arecv[k, j].astype(F32)
+        asum[k] = total.reshape(asum.shape[1:])
+        send_f[k].start()
+
+    def a_finish(k):
+        send_f[k].wait_recv()
+        put(k, gav, asum[k, xl] + frecv[k])
+
+    def b_to_half(k):
+        send_m[k][1].wait_recv()
+        tsend[k] = merged(k, 1, 1 - xl, slice(None)).astype(BF16)
+        send_t[k].start()
+
+    def b_to_owners(k):
+        send_t[k].wait_recv()
+        ysend[k] = (merged(k, 1, xl, slice(None)) + trecv[k].astype(F32)).astype(BF16)
+        for j in (4, 3, 5, 2, 6, 1, 7):
+            send_y[k][j - 1].start()
+
+    def b_finish(k):
+        for j in range(1, NY):
+            send_y[k][j - 1].wait_recv()
+        total = merged(k, 1, xl, y) + trecv[k, y].astype(F32)
+        for j in range(NY - 1):
+            total = total + yrecv[k, j].astype(F32)
+        put(k, gbv, total)
+
+    def put(k, into, total):
         total = total * scale
-        into = (gav, gbv)[h]
         for m in range(2):
             for r in range(8):
                 at = 8 * m + r
@@ -289,58 +298,48 @@
 
     def finish_input(k):
         send_c[k].wait_recv()
-        giv[k] = (own[k] + cr[k].astype(F32)).astype(BF16)
-        store_gi[k].start()
+        giv[:, cols(k)] = (own[k] + cr[k].astype(F32)).astype(BF16)
 
     first_factor(0)
-    to_half(0, 0)
+    a_to_owners(0)
     first_factor(1)
-    to_half(1, 0)
-    pl.semaphore_wait(phase, len(ring))
+    a_to_owners(1)
     for c in send_c[:2]:
         c.start()
     first_factor(2)
     second_factor(0)
-    to_half(2, 0)
-    to_owners(0, 0)
-    to_half(0, 1)
+    a_to_owners(2)
+    b_to_half(0)
     second_factor(1)
-    to_owners(1, 0)
     first_factor(3)
-    to_half(1, 1)
-    to_owners(0, 1)
-    to_half(3, 0)
+    b_to_half(1)
+    b_to_owners(0)
+    a_to_owners(3)
     second_factor(2)
-    to_owners(2, 0)
-    to_half(2, 1)
-    to_owners(1, 1)
-    finish_weights(0, 0)
+    b_to_half(2)
+    b_to_owners(1)
+    a_sum(0)
     second_factor(3)
-    to_owners(3, 0)
-    to_half(3, 1)
-    to_owners(2, 1)
-    finish_weights(1, 0)
-    finish_weights(0, 1)
-    to_owners(3, 1)
-    finish_weights(2, 0)
+    a_sum(1)
+    a_finish(0)
+    b_to_half(3)
+    b_to_owners(2)
+    a_sum(2)
+    b_finish(0)
+    a_finish(1)
+    b_to_owners(3)
+    a_sum(3)
     finish_input(0)
-    finish_weights(1, 1)
-    finish_weights(3, 0)
+    b_finish(1)
+    a_finish(2)
     finish_input(1)
-    finish_weights(2, 1)
+    b_finish(2)
+    a_finish(3)
     finish_input(2)
-    finish_weights(3, 1)
-    store_ga.start()
-    store_gb.start()
+    b_finish(3)
     for k in range(n_blk):
-        for c in [send_x[k], send_p[k], send_h[k], *send_m[k], *send_y[k][0], *send_y[k][1], *send_t[k]]:
+        for c in [send_x[k], send_p[k], send_h[k], *send_m[k], *send_a[k], *send_y[k], send_t[k], send_f[k]]:
             c.wait_send()
-        store_out[k].wait()
-    store_ga.wait()
-    store_gb.wait()
-    for c in store_gi:
-        c.wait()
-    store_own.wait()
     for c in send_c:
         c.wait_send()
     send_c[3].wait_recv()
@@ -364,12 +363,15 @@
     made = pl.pallas_call(
         functools.partial(main_kernel, scale),
         out_shape=(
-            *results,
-            jax.ShapeDtypeStruct((rows, size), F32),
-            jax.ShapeDtypeStruct((rows, size), BF16),
+            pltpu.VMEM((rows, width), BF16),
+            pltpu.VMEM((rows, width - size), BF16),
+            pltpu.VMEM((own_rows, 2, n_blk, size), F32),
+            pltpu.VMEM((own_rows, 2, n_blk, size), F32),
+            pltpu.VMEM((rows, size), F32),
+            pltpu.VMEM((rows, size), BF16),
         ),
         in_specs=[anywhere] * 4,
-        out_specs=[anywhere] * 6,
+        out_specs=[pl.BlockSpec(memory_space=pltpu.VMEM)] * 6,
         scratch_shapes=[
             act,
             act,
@@ -388,16 +390,15 @@
             pltpu.VMEM((n_blk, rows, size), F32),
             pltpu.VMEM((n_blk, 4, 2, NY, 2, own_rows, size), F32),
             pltpu.VMEM((n_blk, 4, 2, NY, own_rows, size), F32),
-            pltpu.VMEM((n_blk, 2, NY, 2 * own_rows, size), BF16),
-            pltpu.VMEM((n_blk, 2, NY - 1, 2 * own_rows, size), BF16),
-            pltpu.VMEM((n_blk, 2, NY, 2 * own_rows, size), BF16),
-            pltpu.VMEM((n_blk, 2, NY, 2 * own_rows, size), BF16),
-            act,
-            act,
-            pltpu.VMEM((own_rows, 2, n_blk, size), F32),
-            pltpu.VMEM((own_rows, 2, n_blk, size), F32),
+            pltpu.VMEM((n_blk, NY, 4 * own_rows, size), BF16),
+            pltpu.VMEM((n_blk, NY - 1, 4 * own_rows, size), BF16),
+            pltpu.VMEM((n_blk, 2, 2 * own_rows, size), F32),
+            pltpu.VMEM((n_blk, 2 * own_rows, size), F32),
+            pltpu.VMEM((n_blk, NY, 2 * own_rows, size), BF16),
+            pltpu.VMEM((n_blk, NY - 1, 2 * own_rows, size), BF16),
+            pltpu.VMEM((n_blk, NY, 2 * own_rows, size), BF16),
+            pltpu.VMEM((n_blk, NY, 2 * own_rows, size), BF16),
             dma((2 * n_blk + 4,)),
-            dma((2 * n_blk + 2,)),
             dma((n_blk,)),
             dma((n_blk,)),
             dma((n_blk,)),
@@ -408,34 +409,45 @@
             dma((n_blk,)),
             dma((n_blk, 2)),
             dma((n_blk, 2)),
-            dma((n_blk, 2, NY - 1)),
-            dma((n_blk, 2, NY - 1)),
-            dma((n_blk, 2)),
-            dma((n_blk, 2)),
-            pltpu.SemaphoreType.REGULAR,
+            dma((n_blk, NY - 1)),
+            dma((n_blk, NY - 1)),
+            dma((n_blk,)),
+            dma((n_blk,)),
+            dma((n_blk, NY - 1)),
+            dma((n_blk, NY - 1)),
+            dma((n_blk,)),
+            dma((n_blk,)),
             pltpu.SemaphoreType.REGULAR,
             pltpu.SemaphoreType.REGULAR,
         ],
         compiler_params=pltpu.CompilerParams(
-            collective_id=0, has_side_effects=True, vmem_limit_bytes=60 << 20
+            collective_id=0, has_side_effects=True, vmem_limit_bytes=40 << 20
         ),
-    )(tokens, upstream, weight_a, weight_b)
-    vm = pl.BlockSpec(memory_space=pltpu.VMEM)
+    )(*[pltpu.with_memory_space_constraint(a, pltpu.HBM) for a in (tokens, upstream, weight_a, weight_b)])
     return pl.pallas_call(
         copy_kernel,
         out_shape=results,
-        in_specs=[vm] * 6,
-        out_specs=[vm] * 4,
-    )(*made)
-
-
-def copy_kernel(out, gi, ga, gb, own, last, out_to, gi_to, ga_to, gb_to):
-    out_to[...] = out[...]
-    ga_to[...] = ga[...]
-    gb_to[...] = gb[...]
-    done = gi.shape[1] - own.shape[1]
-    gi_to[:, :done] = gi[:, :done]
-    gi_to[:, done:] = (own[...] + last[...].astype(F32)).astype(BF16)
+        in_specs=[anywhere] * 4 + [pl.BlockSpec(memory_space=pltpu.VMEM)] * 2,
+        out_specs=[anywhere] * 4,
+        scratch_shapes=[pltpu.VMEM((rows, size), BF16), dma((5,))],
+    )(*[pltpu.with_memory_space_constraint(a, pltpu.VMEM) for a in made])
+
+
+def copy_kernel(out, gi, ga, gb, own, last, out_to, gi_to, ga_to, gb_to, block, sems):
+    done = gi.shape[1]
+    copies = [
+        pltpu.make_async_copy(out, out_to, sems.at[0]),
+        pltpu.make_async_copy(gi, gi_to.at[:, pl.ds(0, done)], sems.at[1]),
+        pltpu.make_async_copy(ga, ga_to, sems.at[2]),
+        pltpu.make_async_copy(gb, gb_to, sems.at[3]),
+        pltpu.make_async_copy(block, gi_to.at[:, pl.ds(done, block.shape[1])], sems.at[4]),
+    ]
+    for c in copies[:4]:
+        c.start()
+    block[...] = (own[...] + last[...].astype(F32)).astype(BF16)
+    copies[4].start()
+    for c in copies:
+        c.wait()
 
 
 def solution(mesh):

time: 63.1 us -> 60.8 us (0.964)
  Pallas kernels: 61.6 us -> 59.9 us
    pallas_call x2, Pallas kernels: 61.6 us -> 59.9 us  [the longest x1 58.9 us: shards(): pl.pallas_call(functools.partial(main_kernel, scale), out_shape=(pltpu.VM...]
where the time goes in v5:
time: 60.8 us; the launch traced here: 60.5 us
  Pallas kernels  59.9 us (99%)
  between operations  0.64 us (1%)
    pallas_call x1, Pallas kernels, shards(): pl.pallas_call(functools.partial(main_kernel, scale), out_shape=(pltpu.VM...  58.9 us

profile of v5, /device:TPU:1, one launch (start us, length us, event | category | flops | bytes accessed | tf_op | source)
XLA Modules:
  0.0 60.5 jit_solution(6001909857691482986)
XLA Ops:
  0.6 58.9 %shard_map.75 = (bf16[256,1024]{1,0:T(8,128)(2,1)S(1)}, bf16[256,768]{1,0:T(8,128)(2,1)S(1)}, f32[8,2,4,256]{3,2,1,0:T(4,128)S(1)}, f32[8,2,4,256]{3,2,1,0:T(4,1...) custom-call(bf16[256,1024]{1,0:T(8,128)(2,1)} %x_hbm.1, bf16[256,1024]{1,0:T(8,128)(2,1)} %g_hbm.1, ...), custom_call_target="tpu_custom_call" | custom-call | tf_op jit(solution)/shard_map/pallas_call | solution.py:363
  59.5 1.0 %shard_map.76 = (bf16[256,1024]{1,0:T(8,128)(2,1)}, bf16[256,1024]{1,0:T(8,128)(2,1)}, f32[8,2,4,256]{3,2,1,0:T(4,128)}, f32[8,2,4,256]{3,2,1,0:T(4,128)}) custom-call(bf16[256,1024]{1,0:T(8,128)(2,1)S(1)} %get-tuple-element.10.out, bf16[256,768]{1,0:T(8,128)(2,1)S(1)} %get-tuple-element.11.gi, f32[8,2,4,256]{3,2,1,0:T(4,128)S(1)} %get-tuple-element.12.ga, ...), custom_call_target="tpu_custom_call" | custom-call | tf_op jit(solution)/shard_map/pallas_call | solution.py:427

commit v6 on v5

--- a/solution.py
+++ b/solution.py
@@ -125,6 +125,12 @@
     ]
     load_wb = [pltpu.make_async_copy(wb_hbm.at[s], wbv.at[s], load_sem.at[2 * n_blk + s]) for s in range(2)]
     load_wa = [pltpu.make_async_copy(wa_hbm.at[s], wav.at[s], load_sem.at[2 * n_blk + 2 + s]) for s in range(2)]
+    pl.semaphore_wait(barrier, jnp.where(low, 1 + len(known), 1))
+
+    send_x = [remote(x_hbm.at[:, cols(k)], xp.at[k], x_ss.at[k], x_rs.at[k], z_dev) for k in range(n_blk)]
+    send_p = [remote(ps.at[k], pr.at[k], p_ss.at[k], p_rs.at[k], xh_dev) for k in range(n_blk)]
+    for c in send_x:
+        c.start()
     load_wb[1].start()
     for c in load_g:
         c.start()
@@ -133,13 +139,6 @@
     load_wa[0].start()
     load_wb[0].start()
     load_wa[1].start()
-
-    pl.semaphore_wait(barrier, jnp.where(low, 1 + len(known), 1))
-
-    send_x = [remote(x_hbm.at[:, cols(k)], xp.at[k], x_ss.at[k], x_rs.at[k], z_dev) for k in range(n_blk)]
-    send_p = [remote(ps.at[k], pr.at[k], p_ss.at[k], p_rs.at[k], xh_dev) for k in range(n_blk)]
-    for c in send_x:
-        c.start()
     @pl.when(low)
     def _():
         for dev in known:
@@ -199,6 +198,8 @@
         remote(asum.at[k, 1 - xl], frecv.at[k], f_ss.at[k], f_rs.at[k], xl_dev) for k in range(n_blk)
     ]
 
+    hold = jnp.where(z == 7, 2, jnp.where(z == 4, 2, jnp.where(z == 2, 3, jnp.where(z == 0, 2, 1))))
+
     def keep(k, m, value):
         loc[k, m] = value.reshape(loc.shape[2:])
 
@@ -227,8 +228,16 @@
         lax.fori_loop(0, size // ROWS, rows, 0)
         send_h[k].start()
         cs[k] = dot_nt(du[k], wav[1, k]).astype(BF16)
-        if k >= 2:
+
+        @pl.when(hold == k)
+        def _():
+            for c in send_c[: k + 1]:
+                c.start()
+
+        @pl.when(hold < k)
+        def _():
             send_c[k].start()
+
         keep(k, 0, dot_tn(xv[k], du[k]))
         keep(k, 1, dot_tn(xp[k], du[k]))
         send_m[k][0].start()
@@ -304,8 +313,6 @@
     a_to_owners(0)
     first_factor(1)
     a_to_owners(1)
-    for c in send_c[:2]:
-        c.start()
     first_factor(2)
     second_factor(0)
     a_to_owners(2)

time: 60.8 us -> 60.3 us (level)
  the two profiles are of different devices: /device:TPU:1 before, /device:TPU:448 now
where the time goes in v6:
time: 60.3 us; the launch traced here: 60.2 us
  Pallas kernels  59.5 us (99%)
  between operations  0.64 us (1%)
    pallas_call x1, Pallas kernels, shards(): pl.pallas_call(functools.partial(main_kernel, scale), out_shape=(pltpu.VM...  58.5 us

profile of v6, /device:TPU:448, one launch (start us, length us, event | category | flops | bytes accessed | tf_op | source)
XLA Modules:
  0.0 60.2 jit_solution(14872108253243885158)
XLA Ops:
  0.6 58.5 %shard_map.75 = (bf16[256,1024]{1,0:T(8,128)(2,1)S(1)}, bf16[256,768]{1,0:T(8,128)(2,1)S(1)}, f32[8,2,4,256]{3,2,1,0:T(4,128)S(1)}, f32[8,2,4,256]{3,2,1,0:T(4,1...) custom-call(bf16[256,1024]{1,0:T(8,128)(2,1)} %x_hbm.1, bf16[256,1024]{1,0:T(8,128)(2,1)} %g_hbm.1, ...), custom_call_target="tpu_custom_call" | custom-call | tf_op jit(solution)/shard_map/pallas_call | solution.py:370
  59.1 1.0 %shard_map.76 = (bf16[256,1024]{1,0:T(8,128)(2,1)}, bf16[256,1024]{1,0:T(8,128)(2,1)}, f32[8,2,4,256]{3,2,1,0:T(4,128)}, f32[8,2,4,256]{3,2,1,0:T(4,128)}) custom-call(bf16[256,1024]{1,0:T(8,128)(2,1)S(1)} %get-tuple-element.10.out, bf16[256,768]{1,0:T(8,128)(2,1)S(1)} %get-tuple-element.11.gi, f32[8,2,4,256]{3,2,1,0:T(4,128)S(1)} %get-tuple-element.12.ga, ...), custom_call_target="tpu_custom_call" | custom-call | tf_op jit(solution)/shard_map/pallas_call | solution.py:434

commit v7 on v6

--- a/solution.py
+++ b/solution.py
@@ -198,7 +198,7 @@
         remote(asum.at[k, 1 - xl], frecv.at[k], f_ss.at[k], f_rs.at[k], xl_dev) for k in range(n_blk)
     ]
 
-    hold = jnp.where(z == 7, 2, jnp.where(z == 4, 2, jnp.where(z == 2, 3, jnp.where(z == 0, 2, 1))))
+    hold = jnp.where(z == 7, 2, jnp.where(z == 5, 2, jnp.where(z == 4, 2, jnp.where(z == 2, 3, jnp.where(z == 0, 2, 1)))))
 
     def keep(k, m, value):
         loc[k, m] = value.reshape(loc.shape[2:])
@@ -310,10 +310,10 @@
         giv[:, cols(k)] = (own[k] + cr[k].astype(F32)).astype(BF16)
 
     first_factor(0)
+    first_factor(1)
     a_to_owners(0)
-    first_factor(1)
+    first_factor(2)
     a_to_owners(1)
-    first_factor(2)
     second_factor(0)
     a_to_owners(2)
     b_to_half(0)

time: 60.3 us -> 59.4 us (0.985)
  the two profiles are of different devices: /device:TPU:448 before, /device:TPU:1 now
where the time goes in v7:
time: 59.4 us; the launch traced here: 58.9 us
  Pallas kernels  58.2 us (98%)
  between operations  0.64 us (1%)
    pallas_call x1, Pallas kernels, shards(): pl.pallas_call(functools.partial(main_kernel, scale), out_shape=(pltpu.VM...  57.2 us

profile of v7, /device:TPU:1, one launch (start us, length us, event | category | flops | bytes accessed | tf_op | source)
XLA Modules:
  0.0 58.9 jit_solution(12829506148872974309)
XLA Ops:
  0.6 57.2 %shard_map.75 = (bf16[256,1024]{1,0:T(8,128)(2,1)S(1)}, bf16[256,768]{1,0:T(8,128)(2,1)S(1)}, f32[8,2,4,256]{3,2,1,0:T(4,128)S(1)}, f32[8,2,4,256]{3,2,1,0:T(4,1...) custom-call(bf16[256,1024]{1,0:T(8,128)(2,1)} %x_hbm.1, bf16[256,1024]{1,0:T(8,128)(2,1)} %g_hbm.1, ...), custom_call_target="tpu_custom_call" | custom-call | tf_op jit(solution)/shard_map/pallas_call | solution.py:370
  57.8 1.0 %shard_map.76 = (bf16[256,1024]{1,0:T(8,128)(2,1)}, bf16[256,1024]{1,0:T(8,128)(2,1)}, f32[8,2,4,256]{3,2,1,0:T(4,128)}, f32[8,2,4,256]{3,2,1,0:T(4,128)}) custom-call(bf16[256,1024]{1,0:T(8,128)(2,1)S(1)} %get-tuple-element.10.out, bf16[256,768]{1,0:T(8,128)(2,1)S(1)} %get-tuple-element.11.gi, f32[8,2,4,256]{3,2,1,0:T(4,128)S(1)} %get-tuple-element.12.ga, ...), custom_call_target="tpu_custom_call" | custom-call | tf_op jit(solution)/shard_map/pallas_call | solution.py:434

commit v8 on v7

--- a/solution.py
+++ b/solution.py
@@ -85,6 +85,8 @@
     t_rs,
     told,
     go,
+    told_x,
+    go_x,
 ):
     n_blk, size = xv.shape[0], xv.shape[1]
     dp, bfly = lax.axis_index("dp"), lax.axis_index("bfly")
@@ -141,8 +143,11 @@
     load_wa[1].start()
     @pl.when(low)
     def _():
+        pl.semaphore_signal(told_x, inc=1, device_id=xh_dev, device_id_type=MESH)
         for dev in known:
             pl.semaphore_signal(told, inc=1, device_id=dev, device_id_type=MESH)
+        pl.semaphore_wait(told_x, 1)
+        pl.semaphore_signal(go_x, inc=1, device_id=z_dev, device_id_type=MESH)
 
     load_wb[1].wait()
     for k in range(n_blk):
@@ -151,7 +156,7 @@
 
     @pl.when(jnp.logical_not(low))
     def _():
-        pl.semaphore_wait(go, 1)
+        pl.semaphore_wait(go_x, 1)
 
     for c in send_p:
         c.start()
@@ -160,6 +165,10 @@
     def _():
         pl.semaphore_wait(told, len(known))
         pl.semaphore_signal(go, inc=1, device_id=z_dev, device_id_type=MESH)
+
+    @pl.when(jnp.logical_not(low))
+    def _():
+        pl.semaphore_wait(go, 1)
 
     send_h = [remote(hv.at[k], hp.at[k], h_ss.at[k], h_rs.at[k], xh_dev) for k in range(n_blk)]
     land_c = [cr.at[k] for k in range(n_blk - 1)] + [last]
@@ -426,6 +435,8 @@
             dma((n_blk,)),
             pltpu.SemaphoreType.REGULAR,
             pltpu.SemaphoreType.REGULAR,
+            pltpu.SemaphoreType.REGULAR,
+            pltpu.SemaphoreType.REGULAR,
         ],
         compiler_params=pltpu.CompilerParams(
             collective_id=0, has_side_effects=True, vmem_limit_bytes=40 << 20

time: 59.4 us -> 59 us (level)
  no operation moved by 1% of the time
where the time goes in v8:
time: 59 us; the launch traced here: 58.8 us
  Pallas kernels  58.1 us (98%)
  between operations  0.64 us (1%)
    pallas_call x1, Pallas kernels, shards(): pl.pallas_call(functools.partial(main_kernel, scale), out_shape=(pltpu.VM...  57.1 us

profile of v8, /device:TPU:1, one launch (start us, length us, event | category | flops | bytes accessed | tf_op | source)
XLA Modules:
  0.0 58.8 jit_solution(15673038175112657229)
XLA Ops:
  0.6 57.1 %shard_map.75 = (bf16[256,1024]{1,0:T(8,128)(2,1)S(1)}, bf16[256,768]{1,0:T(8,128)(2,1)S(1)}, f32[8,2,4,256]{3,2,1,0:T(4,128)S(1)}, f32[8,2,4,256]{3,2,1,0:T(4,1...) custom-call(bf16[256,1024]{1,0:T(8,128)(2,1)} %x_hbm.1, bf16[256,1024]{1,0:T(8,128)(2,1)} %g_hbm.1, ...), custom_call_target="tpu_custom_call" | custom-call | tf_op jit(solution)/shard_map/pallas_call | solution.py:379
  57.7 1.0 %shard_map.76 = (bf16[256,1024]{1,0:T(8,128)(2,1)}, bf16[256,1024]{1,0:T(8,128)(2,1)}, f32[8,2,4,256]{3,2,1,0:T(4,128)}, f32[8,2,4,256]{3,2,1,0:T(4,128)}) custom-call(bf16[256,1024]{1,0:T(8,128)(2,1)S(1)} %get-tuple-element.10.out, bf16[256,768]{1,0:T(8,128)(2,1)S(1)} %get-tuple-element.11.gi, f32[8,2,4,256]{3,2,1,0:T(4,128)S(1)} %get-tuple-element.12.ga, ...), custom_call_target="tpu_custom_call" | custom-call | tf_op jit(solution)/shard_map/pallas_call | solution.py:445

commit v9 on v8

--- a/solution.py
+++ b/solution.py
@@ -339,16 +339,16 @@
     a_sum(1)
     a_finish(0)
     b_to_half(3)
+    finish_input(0)
     b_to_owners(2)
     a_sum(2)
     b_finish(0)
     a_finish(1)
     b_to_owners(3)
     a_sum(3)
-    finish_input(0)
+    finish_input(1)
     b_finish(1)
     a_finish(2)
-    finish_input(1)
     b_finish(2)
     a_finish(3)
     finish_input(2)

time: 59 us -> 59 us (level)
  no operation moved by 1% of the time
where the time goes in v9:
time: 59 us; the launch traced here: 58.8 us
  Pallas kernels  58.1 us (98%)
  between operations  0.64 us (1%)
    pallas_call x1, Pallas kernels, shards(): pl.pallas_call(functools.partial(main_kernel, scale), out_shape=(pltpu.VM...  57.1 us

profile of v9, /device:TPU:1, one launch (start us, length us, event | category | flops | bytes accessed | tf_op | source)
XLA Modules:
  0.0 58.8 jit_solution(16858394663607408877)
XLA Ops:
  0.6 57.1 %shard_map.75 = (bf16[256,1024]{1,0:T(8,128)(2,1)S(1)}, bf16[256,768]{1,0:T(8,128)(2,1)S(1)}, f32[8,2,4,256]{3,2,1,0:T(4,128)S(1)}, f32[8,2,4,256]{3,2,1,0:T(4,1...) custom-call(bf16[256,1024]{1,0:T(8,128)(2,1)} %x_hbm.1, bf16[256,1024]{1,0:T(8,128)(2,1)} %g_hbm.1, ...), custom_call_target="tpu_custom_call" | custom-call | tf_op jit(solution)/shard_map/pallas_call | solution.py:379
  57.7 1.0 %shard_map.76 = (bf16[256,1024]{1,0:T(8,128)(2,1)}, bf16[256,1024]{1,0:T(8,128)(2,1)}, f32[8,2,4,256]{3,2,1,0:T(4,128)}, f32[8,2,4,256]{3,2,1,0:T(4,128)}) custom-call(bf16[256,1024]{1,0:T(8,128)(2,1)S(1)} %get-tuple-element.10.out, bf16[256,768]{1,0:T(8,128)(2,1)S(1)} %get-tuple-element.11.gi, f32[8,2,4,256]{3,2,1,0:T(4,128)S(1)} %get-tuple-element.12.ga, ...), custom_call_target="tpu_custom_call" | custom-call | tf_op jit(solution)/shard_map/pallas_call | solution.py:445
